TPU v7x, 512 devices: a whole 4x4x16 slice. The times are simulated.
512 devices in a mesh: inst: 64 (over x_hi, z, core), tp: 8 (over x_lo, y).
Axes of the slice: x: 4 (x_hi: 2, x_lo: 2; x = x_hi * 2 + x_lo), y: 4, z: 16, core: 2. Of those that a mesh axis runs over, the one named last changes fastest.
Arguments:
- queries: bfloat16 [8192, 8192], P('inst', 'tp'), may hold values from -12 to 12
- span_keys: bfloat16 [8192, 1024], P('inst', 'tp'), may hold values from -12 to 12
- span_values: bfloat16 [8192, 1024], P('inst', 'tp'), may hold values from -6 to 6
- prefix_keys: bfloat16 [4096, 1024], P(('inst', 'tp')), may hold values from -6 to 6
- prefix_values: bfloat16 [4096, 1024], P(('inst', 'tp')), may hold values from -6 to 6
- span_seg: int32 [8192], replicated, may hold values from 0 to 3, never falling along the last dimension, each value on 1 to 4096 neighbouring positions
- prefix_lengths: int32 [4], replicated, may hold values from 1 to 2048, 4096 in all
Outputs:
- attended: bfloat16 [8192, 8192], P('inst', 'tp')
Inputs may be any that keep to these rules, and one draw needn't show every extreme that they name: `span_seg`: requests in order along the block, never falling; each of the 4 requests has 1 to 4096 tokens and one has exactly 4096. `prefix_lengths`: the prefixes lie end to end in request order and sum to 4096; one has exactly 2048.
All inputs are finite; a program needn't handle non-finite values.
Results may differ from a plain program's by a relative error of at most 0.0085.
Values may be sent and summed in bfloat16 or wider, within the bound.
No kernel may reach another device: no remote copies, remote signals or barrier semaphores. Data moves between devices by JAX's collectives and lax.ppermute only.
A program may use at most 128 MiB of HBM per device.

v0:
```python
import math

import jax
import jax.numpy as jnp
from jax import lax
from jax.sharding import PartitionSpec as P

HEADS = 64
KV_HEADS = 8
HD = 128


def body(queries, span_keys, span_values, prefix_keys, prefix_values, span_seg, prefix_lengths):
    inst_place = lax.axis_index("inst")
    q_rows = queries.shape[0]
    kv_local = span_keys.shape[1] // HD
    group = HEADS // KV_HEADS
    scale = 1.0 / math.sqrt(HD)
    cached_k, cached_v = (
        lax.all_to_all(prefix_keys, "tp", split_axis=1, concat_axis=0, tiled=True),
        lax.all_to_all(prefix_values, "tp", split_axis=1, concat_axis=0, tiled=True),
    )
    ends = jnp.cumsum(prefix_lengths)
    starts = ends - prefix_lengths
    row_index = jnp.arange(q_rows, dtype=jnp.int32)
    q_pos = inst_place * q_rows + row_index
    q_seg = jnp.take(span_seg, q_pos)
    low_rows = jnp.take(starts, q_seg)
    high_rows = jnp.take(ends, q_seg)
    query_four = queries.reshape(q_rows, kv_local, group, HD)

    def absorb(state, keys, values, mask):
        top, total, summed = state
        keys_three = keys.reshape(keys.shape[0], kv_local, HD)
        vals_three = values.reshape(values.shape[0], kv_local, HD)
        scores = (
            jnp.einsum("rhgd,chd->rhgc", query_four, keys_three, preferred_element_type=jnp.float32)
            * scale
        )
        scores = jnp.where(mask[:, None, None, :], scores, -jnp.inf)
        new_top = jnp.maximum(top, jnp.max(scores, axis=-1))
        expo = jnp.exp(scores - new_top[..., None])
        factor = jnp.exp(top - new_top)
        total = total * factor + jnp.sum(expo, axis=-1)
        summed = summed * factor[..., None] + jnp.einsum(
            "rhgc,chd->rhgd",
            expo.astype(jnp.bfloat16),
            vals_three,
            preferred_element_type=jnp.float32,
        )
        return (new_top, total, summed)

    start_state = (
        jnp.full((q_rows, kv_local, group), -1e30, jnp.float32),
        jnp.zeros((q_rows, kv_local, group), jnp.float32),
        jnp.zeros((q_rows, kv_local, group, HD), jnp.float32),
    )
    piece = (
        lax.all_gather(cached_k, "inst", axis=0, tiled=True),
        lax.all_gather(cached_v, "inst", axis=0, tiled=True),
    )
    kpos = jnp.arange(piece[0].shape[0], dtype=jnp.int32)
    state = absorb(
        start_state,
        piece[0],
        piece[1],
        (kpos[None, :] >= low_rows[:, None]) & (kpos[None, :] < high_rows[:, None]),
    )
    piece = (
        lax.all_gather(span_keys, "inst", axis=0, tiled=True),
        lax.all_gather(span_values, "inst", axis=0, tiled=True),
    )
    kpos = jnp.arange(piece[0].shape[0], dtype=jnp.int32)
    key_seg = jnp.take(span_seg, kpos)
    state = absorb(
        state,
        piece[0],
        piece[1],
        (key_seg[None, :] == q_seg[:, None]) & (kpos[None, :] <= q_pos[:, None]),
    )
    top, total, summed = state
    result = (summed / total[..., None]).reshape(q_rows, queries.shape[1]).astype(jnp.bfloat16)
    return result


def solution(mesh):
    in_specs = (
        P("inst", "tp"),
        P("inst", "tp"),
        P("inst", "tp"),
        P(("inst", "tp"), None),
        P(("inst", "tp"), None),
        P(),
        P(),
    )
    out_specs = P("inst", "tp")
    return jax.shard_map(body, mesh=mesh, in_specs=in_specs, out_specs=out_specs, check_vma=False)
```

profile of v0, /device:TPU:1, one launch (start us, length us, event | category | flops | bytes accessed | tf_op | source)
XLA Modules:
  0.0 593.4 jit_solution(10841317234310303600)
XLA Ops:
  6.5 11.2 %all_to_all.38 = bf16[8,8,128]{2,0,1:T(8,128)(2,1)} all-to-all(bf16[8,8,128]{2,0,1:T(8,128)(2,1)} %bitcast.143), channel_id=1, replica_groups=mesh['inst'=64,'tp'=8] {'tp'}, dimensions={1} | all-to-all | bytes 32768 | tf_op jit(solution)/shard_map/all_to_all | solution.py:20
  17.8 0.0 all-gather.5.cloned.1.call-update
  17.8 0.0 all-gather.9.cloned.1.call-start
  17.9 0.7 all-gather.9.cloned.1.call-update
  18.6 3.3 all-to-all-start.1
  21.9 0.0 all-gather.11.cloned.1.call-start
  22.0 1.5 copy.17
  23.4 0.0 all-gather.11.cloned.1.call-update
  23.5 0.0 all-gather.7.cloned.1.call-start
  23.6 1.7 gather_fusion
  25.3 0.0 copy-start.3
  25.3 45.5 %gather_fusion.1 = s32[8192]{0:T(1024)S(1)} fusion(s32[8192]{0:T(1024)S(1)} %copy-done.1, s32[8192]{0:T(1024)S(1)} %iota_clamp_fusion), kind=kCustom, calls=%fused_computation.1 | custom fusion | bytes 98304 | tf_op jit(solution)/shard_map/jit(_take)/gather | solution.py:74
  70.8 0.2 reduce-window.9
  71.0 0.7 fusion.63
  71.7 0.7 fusion.62
  72.3 2.5 fusion.54
  74.8 2.5 fusion.55
  77.4 3.7 fusion.14
  81.1 0.5 fusion.18
  81.6 0.6 copy-done.2
  82.2 0.0 all-gather.7.cloned.1.call-update
  82.2 79.5 %all-gather.5.cloned.1.call-done = bf16[4096,128]{1,0:T(8,128)(2,1)} async-done(((bf16[64,128]{1,0:T(8,128)(2,1)}), bf16[4096,128]{1,0:T(8,128)(2,1)}) %all-gather.5.cloned.1.call-update) | async-done | bytes 1048592 | tf_op jit(solution)/shard_map/all_gather | solution.py:59
  161.7 8.2 %fusion.9 = (f32[128,8]{0,1:T(8,128)S(1)}, f32[4096,128,8]{1,0,2:T(8,128)}) fusion(pred[128,4096]{0,1:T(8,128)(4,1)S(1)} %fusion.18, bf16[4096,128]{1,0:T(8,128)(2,1)} %all-gather.5.cloned.1.call-done, bf16[128,1024]{1,0:T(8,128)(2,1)S(1)} %copy-done), kind=kOutput, calls=%fused_computation.14 | convolution fusion | flops 1086323712 | bytes 18616320 | tf_op jit(solution)/shard_map/rhgd,chd->rhgc/dot_general | solution.py:37
  169.9 134.5 %all-gather.9.cloned.1.call-done = bf16[8192,128]{1,0:T(8,128)(2,1)} async-done(((bf16[128,128]{1,0:T(8,128)(2,1)}), bf16[8192,128]{1,0:T(8,128)(2,1)}) %all-gather.9.cloned.1.call-update) | async-done | bytes 2097168 | tf_op jit(solution)/shard_map/all_gather | solution.py:70
  304.4 14.7 %fusion.2 = (f32[128,8]{0,1:T(8,128)S(1)}, f32[8192,128,8]{1,0,2:T(8,128)}) fusion(pred[128,8192]{0,1:T(8,128)(4,1)S(1)} %fusion.14, bf16[8192,128]{1,0:T(8,128)(2,1)} %all-gather.9.cloned.1.call-done, bf16[128,1024]{1,0:T(8,128)(2,1)S(1)} %copy-done), kind=kOutput, calls=%fused_computation.6 | convolution fusion | flops 2172648448 | bytes 36966400 | tf_op jit(solution)/shard_map/rhgd,chd->rhgc/dot_general | solution.py:37
  319.1 9.2 %fusion.7 = f32[128,8]{0,1:T(8,128)S(1)} fusion(f32[4096,128,8]{1,0,2:T(8,128)} %get-tuple-element.22, f32[128,8]{0,1:T(8,128)S(1)} %get-tuple-element.12, pred[128,4096]{0,1:T(8,128)(4,1)S(1)} %fusion.18), kind=kLoop, calls=%fused_computation.12 | loop fusion | flops 16776192 | bytes 17309696 | tf_op jit(solution)/shard_map/reduce_sum | solution.py:44
  328.2 14.2 %fusion = f32[128,8]{0,1:T(8,128)S(1)} fusion(f32[8192,128,8]{1,0,2:T(8,128)} %get-tuple-element.24, f32[128,8]{0,1:T(8,128)S(1)} %get-tuple-element.11, pred[128,8192]{0,1:T(8,128)(4,1)S(1)} %fusion.14), kind=kLoop, calls=%fused_computation.4 | loop fusion | flops 33553408 | bytes 34611200 | tf_op jit(solution)/shard_map/reduce_sum | solution.py:44
  342.5 96.7 %all-gather.11.cloned.1.call-done = bf16[8192,128]{0,1:T(8,128)(2,1)} async-done(((bf16[128,128]{0,1:T(8,128)(2,1)}), bf16[8192,128]{0,1:T(8,128)(2,1)}) %all-gather.11.cloned.1.call-update) | async-done | bytes 2097168 | tf_op jit(solution)/shard_map/all_gather | solution.py:71
  439.2 14.8 %fusion.22 = f32[1,128,128,8]{2,1,3,0:T(8,128)S(1)} fusion(f32[8192,128,8]{1,0,2:T(8,128)} %get-tuple-element.24, f32[128,8]{0,1:T(8,128)S(1)} %get-tuple-element.11, pred[128,8192]{0,1:T(8,128)(4,1)S(1)} %fusion.14, bf16[8192,128]{0,1:T(8,128)(2,1)} %all-gather.11.cloned.1.call-done), kind=kOutput, calls=%fused_computation.27 | convolution fusion | flops 2181038080 | bytes 37228544 | tf_op jit(solution)/shard_map/rhgc,chd->rhgd/dot_general | solution.py:45
  453.9 122.2 %all-gather.7.cloned.1.call-done = bf16[4096,128]{1,0:T(8,128)(2,1)} async-done(((bf16[64,128]{1,0:T(8,128)(2,1)}), bf16[4096,128]{1,0:T(8,128)(2,1)}) %all-gather.7.cloned.1.call-update) | async-done | bytes 1048592 | tf_op jit(solution)/shard_map/all_gather | solution.py:60
  576.1 9.9 %fusion.44 = bf16[1,128,128,8]{2,1,3,0:T(8,128)(2,1)S(1)} fusion(f32[1,128,128,8]{2,1,3,0:T(8,128)S(1)} %fusion.22, bf16[4096,128]{1,0:T(8,128)(2,1)} %all-gather.7.cloned.1.call-done, f32[4096,128,8]{1,0,2:T(8,128)} %get-tuple-element.22, f32[128,8]{0,1:T(8,128)S(1)} %get-tuple-element.12, pred[128,4096]{0,1:T(8,128)(4,1)S(1)} %fusion.18, ...), kind=kOutput, calls=%fused_computation.35 | convolution fusion | flops 1091174400 | bytes 19152896 | tf_op jit(solution)/shard_map/rhgc,chd->rhgd/dot_general | solution.py:45
  586.0 0.9 copy.19
  (16 shorter events, 0.1 us)
Async XLA Ops:
  6.5 155.2 %copy-start = (bf16[128,1024]{1,0:T(8,128)(2,1)S(1)}, bf16[128,1024]{1,0:T(8,128)(2,1)}, u32[]{:S(2)}) copy-start(bf16[128,1024]{1,0:T(8,128)(2,1)} %param.9) | copy-start | bytes 786436
  6.5 18.7 %copy-start.1 = (s32[8192]{0:T(1024)S(1)}, s32[8192]{0:T(1024)}, u32[]{:S(2)}) copy-start(s32[8192]{0:T(1024)} %param.14) | copy-start | bytes 98308
  6.5 155.2 %all-gather.5.cloned.1.call-start = ((), (), s32[]{:S(2)}) async-start(), calls=%async_computation.2 | async-start | bytes 1064960 | tf_op jit(solution)/shard_map/all_gather | solution.py:59
  17.8 286.6 %all-gather.9.cloned.1.call-start = ((), (), s32[]{:S(2)}) async-start(), calls=%async_computation.4 | async-start | bytes 2129920 | tf_op jit(solution)/shard_map/all_gather | solution.py:70
  18.6 63.0 %all-to-all-start.1 = ((bf16[8,8,128]{2,0,1:T(8,128)(2,1)}), bf16[8,8,128]{2,0,1:T(8,128)(2,1)S(1)}, u32[]{:S(2)}, u32[]{:S(2)}) async-start(bf16[8,8,128]{2,0,1:T(8,128)(2,1)} %bitcast.144), calls=%async_computation.1 | async-start | bytes 32768 | tf_op jit(solution)/shard_map/all_to_all | solution.py:21
  21.9 417.2 %all-gather.11.cloned.1.call-start = ((), (), s32[]{:S(2)}) async-start(), calls=%async_computation.5 | async-start | bytes 2129920 | tf_op jit(solution)/shard_map/all_gather | solution.py:71
  23.5 552.6 %all-gather.7.cloned.1.call-start = ((), (), s32[]{:S(2)}) async-start(), calls=%async_computation.3 | async-start | bytes 1064960 | tf_op jit(solution)/shard_map/all_gather | solution.py:60
  25.3 45.6 %copy-start.3 = (s32[4]{0:T(128)S(1)}, s32[4]{0:T(128)}, u32[]{:S(2)}) copy-start(s32[4]{0:T(128)} %param.15) | copy-start | bytes 52
  81.6 0.6 copy-start.2
Sparse Core Ops, SparseCore 0:
  17.9 143.7 all-gather.4
  165.0 139.3 all-gather.8
  307.4 131.7 all-gather.10
  442.3 133.7 all-gather.6
where the time goes:
time: 594 us; the launch traced here: 593 us
  waiting for transfers between devices  434 us (73%)
  local copies, waits for them, and re-layouts  51.5 us (9%)
  matrix products  47.5 us (8%)
  other arithmetic  32.9 us (6%)
  between operations  13.3 us (2%)
  blocking collectives  11.2 us (2%)
    all_gather x1, waiting for transfers between devices, body(): lax.all_gather(span_keys, 'inst', axis=0, tiled=True)  134 us
    all_gather x1, waiting for transfers between devices, body(): lax.all_gather(cached_v, 'inst', axis=0, tiled=True)  122 us
    all_gather x1, waiting for transfers between devices, body(): lax.all_gather(span_values, 'inst', axis=0, tiled=True)  96.7 us
    all_gather x1, waiting for transfers between devices, body(): lax.all_gather(cached_k, 'inst', axis=0, tiled=True)  79.5 us
    gather x1, local copies, waits for them, and re-layouts, body(): key_seg = jnp.take(span_seg, kpos)  45.5 us
    dot_general x2, matrix products, absorb(): jnp.einsum('rhgc,chd->rhgd', expo.astype(jnp.bfloat16), vals_three, prefe...  24.6 us
    reduce_sum x2, other arithmetic, absorb(): total = total * factor + jnp.sum(expo, axis=-1)  23.4 us
    dot_general x2, matrix products, absorb(): jnp.einsum('rhgd,chd->rhgc', query_four, keys_three, preferred_element_ty...  22.9 us
  transfers between devices with their start and end apart: 5, of which 4 were waited for; matrix products, arithmetic and copies ran while one was open for 20% of the time, Pallas kernels for 0%

commit v1 on v0

v1 whole, which is shorter than its diff:
```python
import functools
import math

import jax
import jax.numpy as jnp
from jax import lax
from jax.experimental import pallas as pl
from jax.experimental.pallas import tpu as pltpu
from jax.sharding import Mesh, PartitionSpec as P

HEADS = 64
KV_HEADS = 8
HD = 128
GROUP = HEADS // KV_HEADS
REQ = 4
SPAN = 8192
PREFIX = 4096
XH, Z, CORE, TP = 2, 16, 2, 8
CHIPS = XH * Z
INST = ("xh", "z", "core")
ROWS = SPAN // (CHIPS * CORE)
KEYS = ROWS * CORE
PIECE = PREFIX // CHIPS
BLOCK_ROWS = KEYS + XH * PIECE
LANES = 2 * ROWS
PARTS = GROUP * ROWS // LANES
STEPS = Z // 2
STATE_ROWS = HD + 8
LOW = -1e30
EXP2_SCALE = math.log2(math.e) / math.sqrt(HD)

SMEM = pl.BlockSpec(memory_space=pltpu.SMEM)
VMEM = pl.BlockSpec(memory_space=pltpu.VMEM)
PARAMS = pltpu.CompilerParams(vmem_limit_bytes=24 * 1024 * 1024)


def pack(place_ref, own_ref, first_ref, second_ref, pre_ref, block_ref):
    core = place_ref[2]

    @pl.when(core == 0)
    def _():
        for i, ref in enumerate((own_ref, first_ref)):
            for j in range(2):
                block_ref[i * ROWS : (i + 1) * ROWS, j * HD : (j + 1) * HD] = ref[j]

    @pl.when(core != 0)
    def _():
        for i, ref in enumerate((first_ref, second_ref)):
            for j in range(2):
                block_ref[i * ROWS : (i + 1) * ROWS, j * HD : (j + 1) * HD] = ref[j]

    block_ref[KEYS:, :] = pre_ref[...]


def plan(place_ref, lengths_ref, seg_ref, q_ref, sib_ref, scalars_ref, bounds_ref, rows_ref):
    inst = (place_ref[0] * Z + place_ref[1]) * CORE + place_ref[2]
    sibling = inst + 1 - 2 * place_ref[2]
    seg = seg_ref[...]
    counts = [jnp.int32(0)] + [
        jnp.sum(jnp.where(seg < s, 1.0, 0.0)).astype(jnp.int32) for s in range(1, REQ)
    ]
    starts, ends, running = [], [], jnp.int32(0)
    for s in range(REQ):
        starts.append(running)
        running = running + lengths_ref[s]
        ends.append(running)

    def pick(values, s):
        out = values[0]
        for k in range(1, REQ):
            out = jnp.where(s == k, values[k], out)
        return out

    for half, block in enumerate((inst, sibling)):
        first = block * ROWS
        first_seg, last_seg = jnp.int32(0), jnp.int32(0)
        for s in range(1, REQ):
            first_seg = first_seg + (first >= counts[s]).astype(jnp.int32)
            last_seg = last_seg + (first + ROWS - 1 >= counts[s]).astype(jnp.int32)
        values = (
            pick(starts, first_seg), pick(ends, last_seg), pick(starts, last_seg), pick(ends, first_seg),
            pick(counts, first_seg), first + ROWS, pick(counts, last_seg), first + 1,
        )
        for i, value in enumerate(values):
            scalars_ref[half * 8 + i] = value
        position = first + lax.broadcasted_iota(jnp.int32, (1, ROWS), 1)
        row_seg = jnp.zeros((1, ROWS), jnp.int32)
        for s in range(1, REQ):
            row_seg = row_seg + jnp.where(position >= counts[s], 1, 0)
        bounds_ref[half, 0:1, :] = pick(starts, row_seg)
        bounds_ref[half, 1:2, :] = pick(ends, row_seg)
        bounds_ref[half, 2:3, :] = pick(counts, row_seg)
        bounds_ref[half, 3:4, :] = position + 1
        ref = (q_ref, sib_ref)[half]
        for h in range(GROUP):
            rows_ref[half, h // 2, h % 2 * ROWS : (h % 2 + 1) * ROWS, :] = ref[:, h * HD : (h + 1) * HD]


def absorb_step(step, final, place_ref, scalars_ref, bounds_ref, rows_ref, block_ref, *refs):
    if final:
        before, own_ref, sib_ref, state = refs
        state[...] = before[...]
    elif step:
        before, state = refs
        state[...] = before[...]
    else:
        (state,) = refs
        state[:, :, :HD, :] = jnp.zeros((CORE, PARTS, HD, LANES), jnp.float32)
        state[:, :, HD:, :] = jnp.zeros((CORE, PARTS, STATE_ROWS - HD, LANES), jnp.float32)
        state[:, :, HD : HD + 1, :] = jnp.full((CORE, PARTS, 1, LANES), LOW, jnp.float32)
    core = place_ref[2]
    chip = place_ref[0] * Z + place_ref[1]
    origin = lax.rem(jnp.where(core == 0, chip - step + CHIPS, chip + Z + step), CHIPS)

    def absorb(half, row, count, base, kind, masked):
        keys = block_ref[pl.ds(row, count), :HD]
        vals = block_ref[pl.ds(row, count), HD:]
        if masked:
            index = base + lax.broadcasted_iota(jnp.int32, (count, ROWS), 0)
            low = bounds_ref[half, 2 * kind : 2 * kind + 1, :]
            high = bounds_ref[half, 2 * kind + 1 : 2 * kind + 2, :]
            bias = jnp.where((index >= low) & (index < high), 0.0, LOW)
            bias = jnp.concatenate([bias] * (LANES // ROWS), axis=1)
        for b in range(PARTS):
            scores = lax.dot_general(
                keys, rows_ref[half, b], (((1,), (1,)), ((), ())), preferred_element_type=jnp.float32
            )
            if masked:
                scores = scores + bias
            old = state[half, b, HD : HD + 1, :]
            new = jnp.maximum(old, jnp.max(scores, axis=0, keepdims=True))
            factor = jnp.exp2((old - new) * EXP2_SCALE)
            expo = jnp.exp2((scores - new) * EXP2_SCALE)
            total = state[half, b, HD + 1 : HD + 2, :] * factor + jnp.sum(expo, axis=0, keepdims=True)
            state[half, b, HD : HD + 1, :] = new
            state[half, b, HD + 1 : HD + 2, :] = total
            state[half, b, :HD, :] = state[half, b, :HD, :] * factor + lax.dot_general(
                vals, expo.astype(jnp.bfloat16), (((0,), (0,)), ((), ())), preferred_element_type=jnp.float32
            )

    def visit(half, row, count, base, kind, wanted):
        least_lo, most_hi, most_lo, least_hi = [scalars_ref[half * 8 + kind * 4 + i] for i in range(4)]
        seen = wanted & (base < most_hi) & (base + count > least_lo)
        whole = (base >= most_lo) & (base + count <= least_hi)

        @pl.when(seen & whole)
        def _():
            absorb(half, row, count, base, kind, False)

        @pl.when(seen & jnp.logical_not(whole))
        def _():
            absorb(half, row, count, base, kind, True)

    def one_half(half, carry):
        visit(half, 0, KEYS, origin * KEYS, 1, (core == 0) | (step < STEPS))

        def one_piece(xh, carry):
            row = pl.multiple_of(KEYS + xh * PIECE, PIECE)
            base = (xh * Z + lax.rem(origin, Z)) * PIECE
            visit(half, row, PIECE, base, 0, (core == 0) | (0 < step < STEPS))
            return carry

        return lax.fori_loop(0, XH, one_piece, carry)

    lax.fori_loop(0, CORE, one_half, 0)
    if final:
        own_ref[...] = state[0]
        sib_ref[...] = state[1]


def merge(own_ref, other_ref, out_ref):
    for b in range(PARTS):
        top_a, top_b = own_ref[b, HD : HD + 1, :], other_ref[b, HD : HD + 1, :]
        top = jnp.maximum(top_a, top_b)
        factor_a = jnp.exp2((top_a - top) * EXP2_SCALE)
        factor_b = jnp.exp2((top_b - top) * EXP2_SCALE)
        total = own_ref[b, HD + 1 : HD + 2, :] * factor_a + other_ref[b, HD + 1 : HD + 2, :] * factor_b
        result = (own_ref[b, :HD, :] * factor_a + other_ref[b, :HD, :] * factor_b) / total
        for i in range(LANES // ROWS):
            h = b * (LANES // ROWS) + i
            out_ref[:, h * HD : (h + 1) * HD] = result[:, i * ROWS : (i + 1) * ROWS].T.astype(jnp.bfloat16)


STATE = jax.ShapeDtypeStruct((CORE, PARTS, STATE_ROWS, LANES), jnp.float32)
HALF_STATE = jax.ShapeDtypeStruct((PARTS, STATE_ROWS, LANES), jnp.float32)


def call_pack(place, own, first, second, pre):
    return pl.pallas_call(
        pack,
        out_shape=jax.ShapeDtypeStruct((BLOCK_ROWS, 2 * HD), jnp.bfloat16),
        in_specs=[SMEM, VMEM, VMEM, VMEM, VMEM],
        out_specs=VMEM,
        compiler_params=PARAMS,
        name="pack",
    )(place, own, first, second, pre)


def call_plan(place, prefix_lengths, span_seg, queries, sib_queries):
    return pl.pallas_call(
        plan,
        out_shape=(
            jax.ShapeDtypeStruct((CORE * 8,), jnp.int32),
            jax.ShapeDtypeStruct((CORE, 8, ROWS), jnp.int32),
            jax.ShapeDtypeStruct((CORE, PARTS, LANES, HD), jnp.bfloat16),
        ),
        in_specs=[SMEM, SMEM, VMEM, VMEM, VMEM],
        out_specs=(SMEM, VMEM, VMEM),
        compiler_params=PARAMS,
        name="plan",
    )(place, prefix_lengths, span_seg.reshape(-1, ROWS), queries, sib_queries)


def call_absorb(step, place, planned, block, state):
    final = step == STEPS
    return pl.pallas_call(
        functools.partial(absorb_step, step, final),
        out_shape=(HALF_STATE, HALF_STATE) if final else STATE,
        in_specs=[SMEM, SMEM, VMEM, VMEM, VMEM] + ([VMEM] if step else []),
        out_specs=(VMEM, VMEM) if final else VMEM,
        scratch_shapes=[pltpu.VMEM(STATE.shape, STATE.dtype)] if final else [],
        compiler_params=PARAMS,
        cost_estimate=pl.CostEstimate(flops=537_000_000, bytes_accessed=3_000_000, transcendentals=1_050_000),
        name="absorb",
    )(place, *planned, block, *([state] if step else []))


def call_merge(own, other):
    return pl.pallas_call(
        merge,
        out_shape=jax.ShapeDtypeStruct((ROWS, GROUP * HD), jnp.bfloat16),
        in_specs=[VMEM, VMEM],
        out_specs=VMEM,
        compiler_params=PARAMS,
        name="merge",
    )(own, other)


def at(xh, z, core):
    return (xh * Z + z) * CORE + core


def body(queries, span_keys, span_values, prefix_keys, prefix_values, span_seg, prefix_lengths):
    place = jnp.stack([lax.axis_index(a) for a in INST]).astype(jnp.int32)
    everyone = [(xh, z) for xh in range(XH) for z in range(Z)]
    cores = [(at(xh, z, c), at(xh, z, 1 - c)) for xh, z in everyone for c in range(CORE)]
    one = [(at(xh, z, 1), at(xh, z, 0)) for xh, z in everyone] + [(at(xh, z, 0), at(1 - xh, z, 1)) for xh, z in everyone]
    two = [(at(xh, z, 1), at(1 - xh, z, 1)) for xh, z in everyone]
    onward = [(c * CORE, (c + 1) % CHIPS * CORE) for c in range(CHIPS)]
    back = [(c * CORE + 1, (c - 1) % CHIPS * CORE + 1) for c in range(CHIPS)]

    span = jnp.stack([span_keys, span_values])
    first = lax.ppermute(span, INST, one)
    second = lax.ppermute(span, INST, two)
    sib_queries = lax.ppermute(queries, INST, cores)

    pre = jnp.concatenate(
        [prefix_keys.reshape(-1, KV_HEADS, HD), prefix_values.reshape(-1, KV_HEADS, HD)], axis=2
    ).transpose(1, 0, 2)
    pre = jnp.broadcast_to(pre[None], (XH * CORE,) + pre.shape).reshape((XH * CORE * TP,) + pre.shape[1:])
    pre = lax.all_to_all(pre, ("xh", "core", "tp"), split_axis=0, concat_axis=0, tiled=True)
    pre = pre.reshape(XH * PIECE, 2 * HD)

    block = call_pack(place, span, first, second, pre)
    planned = call_plan(place, prefix_lengths, span_seg, queries, sib_queries)
    state = None
    for step in range(STEPS + 1):
        if step < STEPS:
            arriving = lax.ppermute(block, INST, onward + back if step < STEPS - 1 else onward)
        state = call_absorb(step, place, planned, block, state)
        if step < STEPS:
            block, state = lax.optimization_barrier((arriving, state))
    own, sib = state
    return call_merge(own, lax.ppermute(sib, INST, cores))


def solution(mesh):
    cut = Mesh(mesh.devices.reshape(XH, Z, CORE, TP), INST + ("tp",))
    in_specs = (
        P(INST, "tp"),
        P(INST, "tp"),
        P(INST, "tp"),
        P(INST + ("tp",), None),
        P(INST + ("tp",), None),
        P(),
        P(),
    )
    return jax.shard_map(body, mesh=cut, in_specs=in_specs, out_specs=P(INST, "tp"), check_vma=False)
```

time: 594 us -> 129 us (0.22)
  waiting for transfers between devices: 434 us -> 12.5 us
  starting transfers between devices: 3.48 us -> 94.6 us
  local copies, waits for them, and re-layouts: 51.5 us -> 0.68 us
  matrix products: 47.5 us -> 0 us
  other arithmetic: 32.9 us -> 1.64 us
  Pallas kernels: 0 us -> 19 us
  between operations: 13.3 us -> 0.25 us
  blocking collectives: 11.2 us -> 0 us
    all_gather x4 -> x0, waiting for transfers between devices: 433 us -> none  [the longest x1 134 us: body(): lax.all_gather(span_keys, 'inst', axis=0, tiled=True)]
    ppermute x0 -> x12, starting transfers between devices: none -> 84.1 us  [the longest x8 54.7 us: body(): lax.ppermute(block, INST, onward + back if step < STEPS - 1 else onward)]
    gather x4 -> x0, local copies, waits for them, and re-layouts: 48.5 us -> none  [the longest x1 45.5 us: body(): key_seg = jnp.take(span_seg, kpos)]
    dot_general x4 -> x0, matrix products: 47.5 us -> none  [the longest x2 24.6 us: absorb(): jnp.einsum('rhgc,chd->rhgd', expo.astype(jnp.bfloat16), vals_three, prefe...]
    reduce_sum x2 -> x0, other arithmetic: 23.4 us -> none  [absorb(): total = total * factor + jnp.sum(expo, axis=-1)]
    pallas_call x0 -> x12, Pallas kernels: none -> 19 us  [the longest x9 16.2 us: call_absorb(): pl.pallas_call(functools.partial(absorb_step, step, final), out_shape=(HA...]
    ppermute x0 -> x12, waiting for transfers between devices: none -> 12.5 us  [the longest x8 8.18 us: body(): lax.ppermute(block, INST, onward + back if step < STEPS - 1 else onward)]
    all_to_all x1 -> x0, blocking collectives: 11.2 us -> none  [body(): lax.all_to_all(prefix_keys, 'tp', split_axis=1, concat_axis=0, tiled=True)]
  transfers between devices with their start and end apart: 5 -> 13, of which waited for: 4 -> 9; matrix products, arithmetic and copies ran while one was open for 20% -> 1% of each run, Pallas kernels for 0% -> 13%
where the time goes in v1:
time: 129 us
  starting transfers between devices  94.6 us (73%)
  Pallas kernels  19 us (15%)
  waiting for transfers between devices  12.5 us (10%)
  other arithmetic  1.64 us (1%)
    ppermute x8, starting transfers between devices, body(): lax.ppermute(block, INST, onward + back if step < STEPS - 1 else onward)  54.7 us
    ppermute x1, starting transfers between devices, body(): return call_merge(own, lax.ppermute(sib, INST, cores))  20.3 us
    pallas_call x9, Pallas kernels, call_absorb(): pl.pallas_call(functools.partial(absorb_step, step, final), out_shape=(HA...  16.2 us
    all_to_all x1, starting transfers between devices, body(): lax.all_to_all(pre, ('xh', 'core', 'tp'), split_axis=0, concat_axis=0, ti...  10.4 us
    ppermute x8, waiting for transfers between devices, body(): lax.ppermute(block, INST, onward + back if step < STEPS - 1 else onward)  8.18 us
    ppermute x1, starting transfers between devices, body(): second = lax.ppermute(span, INST, two)  4.86 us
    ppermute x1, waiting for transfers between devices, body(): first = lax.ppermute(span, INST, one)  2.76 us
  transfers between devices with their start and end apart: 13, of which 9 were waited for; matrix products, arithmetic and copies ran while one was open for 1% of the time, Pallas kernels for 13%

profile of v1, /device:TPU:1, one launch (start us, length us, event | category | flops | bytes accessed | tf_op | source)
XLA Modules:
  0.0 128.6 jit_solution(17903048701056492949)
XLA Ops:
  1.5 10.4 %all-to-all-start = ((bf16[32,8,256]{2,1,0:T(8,128)(2,1)}), bf16[32,8,256]{2,1,0:T(8,128)(2,1)S(1)}, u32[]{:S(2)}, u32[]{:S(2)}) async-start(bf16[32,8,256]{2,1,0:T(8,128)(2,1)} %bitcast.9), calls=%async_computation | async-start | bytes 262144 | tf_op jit(solution)/shard_map/all_to_all | solution.py:261
  12.7 4.9 %collective-permute-start.2 = (bf16[2,128,128]{2,1,0:T(8,128)(2,1)S(1)}, bf16[2,128,128]{2,1,0:T(8,128)(2,1)S(1)}, u32[]{:S(2)}, u32[]{:S(2)}) collective-permute-start(bf16[2,128,128]{2,1,0:T(8,128)(2,1)S(1)} %pad_maximum_fusion.own_ref), channel_id=1, source_target_pairs={{8,264},{24,280},{40,296},{56,312},{72,328},{88,344},{104,360},{12... | collective-permute-start | bytes 196616 | tf_op jit(solution)/shard_map/ppermute | solution.py:254
  17.6 1.9 %collective-permute-start.1 = (bf16[2,128,128]{2,1,0:T(8,128)(2,1)S(1)}, bf16[2,128,128]{2,1,0:T(8,128)(2,1)S(1)}, u32[]{:S(2)}, u32[]{:S(2)}) collective-permute-start(bf16[2,128,128]{2,1,0:T(8,128)(2,1)S(1)} %pad_maximum_fusion.own_ref), channel_id=1, source_target_pairs={{8,0},{24,16},{40,32},{56,48},{72,64},{88,80},{104,96},{120,112},{... | collective-permute-start | bytes 196616 | tf_op jit(solution)/shard_map/ppermute | solution.py:253
  19.5 2.3 %collective-permute-start = (bf16[128,1024]{1,0:T(8,128)(2,1)}, bf16[128,1024]{1,0:T(8,128)(2,1)S(1)}, u32[]{:S(2)}, u32[]{:S(2)}) collective-permute-start(bf16[128,1024]{1,0:T(8,128)(2,1)} %q_ref.1), channel_id=1, source_target_pairs={{0,8},{8,0},{16,24},{24,16},{32,40},{40,32},{48,56},{56,48},{64,72... | collective-permute-start | bytes 786440 | tf_op jit(solution)/shard_map/ppermute | solution.py:255
  21.9 2.8 %collective-permute-done.1.first_ref = bf16[2,128,128]{2,1,0:T(8,128)(2,1)S(1)} collective-permute-done((bf16[2,128,128]{2,1,0:T(8,128)(2,1)S(1)}, bf16[2,128,128]{2,1,0:T(8,128)(2,1)S(1)}, u32[]{:S(2)}, u32[]{:S(2)}) %collective-permute-start.1) | collective-permute-done | bytes 65568 | tf_op jit(solution)/shard_map/ppermute | solution.py:253
  25.2 9.1 %collective-permute-start.3 = (bf16[512,256]{1,0:T(8,128)(2,1)S(1)}, bf16[512,256]{1,0:T(8,128)(2,1)S(1)}, u32[]{:S(2)}, u32[]{:S(2)}) collective-permute-start(bf16[512,256]{1,0:T(8,128)(2,1)S(1)} %pack.1.block_ref), channel_id=1, source_target_pairs={{0,16},{16,32},{32,48},{48,64},{64,80},{80,96},{96,112},{112,128},... | collective-permute-start | bytes 786440 | tf_op jit(solution)/shard_map/ppermute | solution.py:269
  34.4 1.3 %plan.1 = (s32[16]{0:T(128)S(1)}, s32[2,8,128]{2,1,0:T(8,128)S(1)}, bf16[2,4,256,128]{3,2,1,0:T(8,128)(2,1)S(1)}) custom-call(s32[3]{0:T(128)S(1)} %pad_add_fusion.place_ref, s32[4]{0:T(128)S(1)} %copy-done.2, s32[64,128]{1,0:T(8,128)S(1)} %bitcast.13, bf16[128,1024]{1,0:T(8,128)(2,1)S(1)} %copy-done, bf16[128,1024]{1,0:T(8,128)(2,1)S(1)} %collective-permute-done.sib_ref), custom_call_target="tpu_custom_call" | custom-call | tf_op jit(solution)/shard_map/plan/pallas_call | solution.py:200
  36.5 1.2 collective-permute-done.3.block_ref
  37.7 7.4 %collective-permute-start.4 = (bf16[512,256]{1,0:T(8,128)(2,1)S(1)}, bf16[512,256]{1,0:T(8,128)(2,1)S(1)}, u32[]{:S(2)}, u32[]{:S(2)}) collective-permute-start(bf16[512,256]{1,0:T(8,128)(2,1)S(1)} %collective-permute-done.3.block_ref), channel_id=1, source_target_pairs={{0,16},{16,32},{32,48},{48,64},{64,80},{80,96},{96,112},{112,128},... | collective-permute-start | bytes 786440 | tf_op jit(solution)/shard_map/ppermute | solution.py:269
  45.1 2.1 %absorb.10.refs_0_ = f32[2,4,136,256]{3,2,1,0:T(8,128)S(1)} custom-call(s32[3]{0:T(128)S(1)} %pad_add_fusion.place_ref, s32[16]{0:T(128)S(1)} %get-tuple-element.26.scalars_ref, s32[2,8,128]{2,1,0:T(8,128)S(1)} %get-tuple-element.27.bounds_ref, bf16[2,4,256,128]{3,2,1,0:T(8,128)(2,1)S(1)} %get-tuple-element.28.rows_ref, ...), custom_call_target="tpu_custom_call" | custom-call | flops 537000000 | bytes 3000000 | tf_op jit(solution)/shard_map/absorb/pallas_call | solution.py:216
  47.2 1.2 collective-permute-done.4.block_ref
  48.4 7.4 %collective-permute-start.5 = (bf16[512,256]{1,0:T(8,128)(2,1)S(1)}, bf16[512,256]{1,0:T(8,128)(2,1)S(1)}, u32[]{:S(2)}, u32[]{:S(2)}) collective-permute-start(bf16[512,256]{1,0:T(8,128)(2,1)S(1)} %collective-permute-done.4.block_ref), channel_id=1, source_target_pairs={{0,16},{16,32},{32,48},{48,64},{64,80},{80,96},{96,112},{112,128},... | collective-permute-start | bytes 786440 | tf_op jit(solution)/shard_map/ppermute | solution.py:269
  55.8 2.1 %absorb.11.refs_0_ = f32[2,4,136,256]{3,2,1,0:T(8,128)S(1)} custom-call(s32[3]{0:T(128)S(1)} %pad_add_fusion.place_ref, s32[16]{0:T(128)S(1)} %get-tuple-element.26.scalars_ref, s32[2,8,128]{2,1,0:T(8,128)S(1)} %get-tuple-element.27.bounds_ref, bf16[2,4,256,128]{3,2,1,0:T(8,128)(2,1)S(1)} %get-tuple-element.28.rows_ref, ...), custom_call_target="tpu_custom_call" | custom-call | flops 537000000 | bytes 3000000 | tf_op jit(solution)/shard_map/absorb/pallas_call | solution.py:216
  57.9 1.2 collective-permute-done.5.block_ref
  59.1 7.4 %collective-permute-start.6 = (bf16[512,256]{1,0:T(8,128)(2,1)S(1)}, bf16[512,256]{1,0:T(8,128)(2,1)S(1)}, u32[]{:S(2)}, u32[]{:S(2)}) collective-permute-start(bf16[512,256]{1,0:T(8,128)(2,1)S(1)} %collective-permute-done.5.block_ref), channel_id=1, source_target_pairs={{0,16},{16,32},{32,48},{48,64},{64,80},{80,96},{96,112},{112,128},... | collective-permute-start | bytes 786440 | tf_op jit(solution)/shard_map/ppermute | solution.py:269
  66.5 2.1 %absorb.12.refs_0_ = f32[2,4,136,256]{3,2,1,0:T(8,128)S(1)} custom-call(s32[3]{0:T(128)S(1)} %pad_add_fusion.place_ref, s32[16]{0:T(128)S(1)} %get-tuple-element.26.scalars_ref, s32[2,8,128]{2,1,0:T(8,128)S(1)} %get-tuple-element.27.bounds_ref, bf16[2,4,256,128]{3,2,1,0:T(8,128)(2,1)S(1)} %get-tuple-element.28.rows_ref, ...), custom_call_target="tpu_custom_call" | custom-call | flops 537000000 | bytes 3000000 | tf_op jit(solution)/shard_map/absorb/pallas_call | solution.py:216
  68.6 1.2 collective-permute-done.6.block_ref
  69.8 7.6 %collective-permute-start.7 = (bf16[512,256]{1,0:T(8,128)(2,1)S(1)}, bf16[512,256]{1,0:T(8,128)(2,1)S(1)}, u32[]{:S(2)}, u32[]{:S(2)}) collective-permute-start(bf16[512,256]{1,0:T(8,128)(2,1)S(1)} %collective-permute-done.6.block_ref), channel_id=1, source_target_pairs={{0,16},{16,32},{32,48},{48,64},{64,80},{80,96},{96,112},{112,128},... | collective-permute-start | bytes 786440 | tf_op jit(solution)/shard_map/ppermute | solution.py:269
  77.4 2.1 %absorb.13.refs_0_ = f32[2,4,136,256]{3,2,1,0:T(8,128)S(1)} custom-call(s32[3]{0:T(128)S(1)} %pad_add_fusion.place_ref, s32[16]{0:T(128)S(1)} %get-tuple-element.26.scalars_ref, s32[2,8,128]{2,1,0:T(8,128)S(1)} %get-tuple-element.27.bounds_ref, bf16[2,4,256,128]{3,2,1,0:T(8,128)(2,1)S(1)} %get-tuple-element.28.rows_ref, ...), custom_call_target="tpu_custom_call" | custom-call | flops 537000000 | bytes 3000000 | tf_op jit(solution)/shard_map/absorb/pallas_call | solution.py:216
  79.5 1.0 collective-permute-done.7.block_ref
  80.6 7.4 %collective-permute-start.8 = (bf16[512,256]{1,0:T(8,128)(2,1)S(1)}, bf16[512,256]{1,0:T(8,128)(2,1)S(1)}, u32[]{:S(2)}, u32[]{:S(2)}) collective-permute-start(bf16[512,256]{1,0:T(8,128)(2,1)S(1)} %collective-permute-done.7.block_ref), channel_id=1, source_target_pairs={{0,16},{16,32},{32,48},{48,64},{64,80},{80,96},{96,112},{112,128},... | collective-permute-start | bytes 786440 | tf_op jit(solution)/shard_map/ppermute | solution.py:269
  88.0 2.1 %absorb.14.refs_0_ = f32[2,4,136,256]{3,2,1,0:T(8,128)S(1)} custom-call(s32[3]{0:T(128)S(1)} %pad_add_fusion.place_ref, s32[16]{0:T(128)S(1)} %get-tuple-element.26.scalars_ref, s32[2,8,128]{2,1,0:T(8,128)S(1)} %get-tuple-element.27.bounds_ref, bf16[2,4,256,128]{3,2,1,0:T(8,128)(2,1)S(1)} %get-tuple-element.28.rows_ref, ...), custom_call_target="tpu_custom_call" | custom-call | flops 537000000 | bytes 3000000 | tf_op jit(solution)/shard_map/absorb/pallas_call | solution.py:216
  90.1 1.2 collective-permute-done.8.block_ref
  91.3 7.4 %collective-permute-start.9 = (bf16[512,256]{1,0:T(8,128)(2,1)S(1)}, bf16[512,256]{1,0:T(8,128)(2,1)S(1)}, u32[]{:S(2)}, u32[]{:S(2)}) collective-permute-start(bf16[512,256]{1,0:T(8,128)(2,1)S(1)} %collective-permute-done.8.block_ref), channel_id=1, source_target_pairs={{0,16},{16,32},{32,48},{48,64},{64,80},{80,96},{96,112},{112,128},... | collective-permute-start | bytes 786440 | tf_op jit(solution)/shard_map/ppermute | solution.py:269
  98.7 2.1 %absorb.15.refs_0_ = f32[2,4,136,256]{3,2,1,0:T(8,128)S(1)} custom-call(s32[3]{0:T(128)S(1)} %pad_add_fusion.place_ref, s32[16]{0:T(128)S(1)} %get-tuple-element.26.scalars_ref, s32[2,8,128]{2,1,0:T(8,128)S(1)} %get-tuple-element.27.bounds_ref, bf16[2,4,256,128]{3,2,1,0:T(8,128)(2,1)S(1)} %get-tuple-element.28.rows_ref, ...), custom_call_target="tpu_custom_call" | custom-call | flops 537000000 | bytes 3000000 | tf_op jit(solution)/shard_map/absorb/pallas_call | solution.py:216
  100.8 1.2 collective-permute-done.9.block_ref
  102.0 0.9 collective-permute-start.10
  102.9 2.1 %absorb.16.refs_0_ = f32[2,4,136,256]{3,2,1,0:T(8,128)S(1)} custom-call(s32[3]{0:T(128)S(1)} %pad_add_fusion.place_ref, s32[16]{0:T(128)S(1)} %get-tuple-element.26.scalars_ref, s32[2,8,128]{2,1,0:T(8,128)S(1)} %get-tuple-element.27.bounds_ref, bf16[2,4,256,128]{3,2,1,0:T(8,128)(2,1)S(1)} %get-tuple-element.28.rows_ref, ...), custom_call_target="tpu_custom_call" | custom-call | flops 537000000 | bytes 3000000 | tf_op jit(solution)/shard_map/absorb/pallas_call | solution.py:216
  105.0 0.8 absorb.17
  105.8 20.3 %collective-permute-start.11 = (f32[4,136,256]{2,1,0:T(8,128)S(1)}, f32[4,136,256]{2,1,0:T(8,128)S(1)}, u32[]{:S(2)}, u32[]{:S(2)}) collective-permute-start(f32[4,136,256]{2,1,0:T(8,128)S(1)} %get-tuple-element.46), channel_id=1, source_target_pairs={{0,8},{8,0},{16,24},{24,16},{32,40},{40,32},{48,56},{56,48},{64,72... | collective-permute-start | bytes 1671176 | tf_op jit(solution)/shard_map/ppermute | solution.py:274
  126.2 1.6 %collective-permute-done.11.other_ref = f32[4,136,256]{2,1,0:T(8,128)S(1)} collective-permute-done((f32[4,136,256]{2,1,0:T(8,128)S(1)}, f32[4,136,256]{2,1,0:T(8,128)S(1)}, u32[]{:S(2)}, u32[]{:S(2)}) %collective-permute-start.11) | collective-permute-done | bytes 557088 | tf_op jit(solution)/shard_map/ppermute | solution.py:274
  127.7 0.9 merge.1
  (16 shorter events, 3.7 us)
Async XLA Ops:
  0.0 34.4 %copy-start = (bf16[128,1024]{1,0:T(8,128)(2,1)S(1)}, bf16[128,1024]{1,0:T(8,128)(2,1)}, u32[]{:S(2)}) copy-start(bf16[128,1024]{1,0:T(8,128)(2,1)} %q_ref.1) | copy-start | bytes 786436
  0.0 34.4 %copy-start.2 = (s32[4]{0:T(128)S(1)}, s32[4]{0:T(128)}, u32[]{:S(2)}) copy-start(s32[4]{0:T(128)} %lengths_ref.1) | copy-start | bytes 52
  0.0 34.4 %copy-start.1 = (s32[8192]{0:T(1024)S(1)}, s32[8192]{0:T(1024)}, u32[]{:S(2)}) copy-start(s32[8192]{0:T(1024)} %param.12) | copy-start | bytes 98308
  1.5 23.2 %all-to-all-start = ((bf16[32,8,256]{2,1,0:T(8,128)(2,1)}), bf16[32,8,256]{2,1,0:T(8,128)(2,1)S(1)}, u32[]{:S(2)}, u32[]{:S(2)}) async-start(bf16[32,8,256]{2,1,0:T(8,128)(2,1)} %bitcast.9), calls=%async_computation | async-start | bytes 262144 | tf_op jit(solution)/shard_map/all_to_all | solution.py:261
  12.7 9.2 %collective-permute-start.2 = (bf16[2,128,128]{2,1,0:T(8,128)(2,1)S(1)}, bf16[2,128,128]{2,1,0:T(8,128)(2,1)S(1)}, u32[]{:S(2)}, u32[]{:S(2)}) collective-permute-start(bf16[2,128,128]{2,1,0:T(8,128)(2,1)S(1)} %pad_maximum_fusion.own_ref), channel_id=1, source_target_pairs={{8,264},{24,280},{40,296},{56,312},{72,328},{88,344},{104,360},{12... | collective-permute-start | bytes 196616 | tf_op jit(solution)/shard_map/ppermute | solution.py:254
  17.6 7.1 %collective-permute-start.1 = (bf16[2,128,128]{2,1,0:T(8,128)(2,1)S(1)}, bf16[2,128,128]{2,1,0:T(8,128)(2,1)S(1)}, u32[]{:S(2)}, u32[]{:S(2)}) collective-permute-start(bf16[2,128,128]{2,1,0:T(8,128)(2,1)S(1)} %pad_maximum_fusion.own_ref), channel_id=1, source_target_pairs={{8,0},{24,16},{40,32},{56,48},{72,64},{88,80},{104,96},{120,112},{... | collective-permute-start | bytes 196616 | tf_op jit(solution)/shard_map/ppermute | solution.py:253
  19.5 14.9 %collective-permute-start = (bf16[128,1024]{1,0:T(8,128)(2,1)}, bf16[128,1024]{1,0:T(8,128)(2,1)S(1)}, u32[]{:S(2)}, u32[]{:S(2)}) collective-permute-start(bf16[128,1024]{1,0:T(8,128)(2,1)} %q_ref.1), channel_id=1, source_target_pairs={{0,8},{8,0},{16,24},{24,16},{32,40},{40,32},{48,56},{56,48},{64,72... | collective-permute-start | bytes 786440 | tf_op jit(solution)/shard_map/ppermute | solution.py:255
  25.2 12.4 %collective-permute-start.3 = (bf16[512,256]{1,0:T(8,128)(2,1)S(1)}, bf16[512,256]{1,0:T(8,128)(2,1)S(1)}, u32[]{:S(2)}, u32[]{:S(2)}) collective-permute-start(bf16[512,256]{1,0:T(8,128)(2,1)S(1)} %pack.1.block_ref), channel_id=1, source_target_pairs={{0,16},{16,32},{32,48},{48,64},{64,80},{80,96},{96,112},{112,128},... | collective-permute-start | bytes 786440 | tf_op jit(solution)/shard_map/ppermute | solution.py:269
  37.7 10.7 %collective-permute-start.4 = (bf16[512,256]{1,0:T(8,128)(2,1)S(1)}, bf16[512,256]{1,0:T(8,128)(2,1)S(1)}, u32[]{:S(2)}, u32[]{:S(2)}) collective-permute-start(bf16[512,256]{1,0:T(8,128)(2,1)S(1)} %collective-permute-done.3.block_ref), channel_id=1, source_target_pairs={{0,16},{16,32},{32,48},{48,64},{64,80},{80,96},{96,112},{112,128},... | collective-permute-start | bytes 786440 | tf_op jit(solution)/shard_map/ppermute | solution.py:269
  48.4 10.7 %collective-permute-start.5 = (bf16[512,256]{1,0:T(8,128)(2,1)S(1)}, bf16[512,256]{1,0:T(8,128)(2,1)S(1)}, u32[]{:S(2)}, u32[]{:S(2)}) collective-permute-start(bf16[512,256]{1,0:T(8,128)(2,1)S(1)} %collective-permute-done.4.block_ref), channel_id=1, source_target_pairs={{0,16},{16,32},{32,48},{48,64},{64,80},{80,96},{96,112},{112,128},... | collective-permute-start | bytes 786440 | tf_op jit(solution)/shard_map/ppermute | solution.py:269
  59.1 10.7 %collective-permute-start.6 = (bf16[512,256]{1,0:T(8,128)(2,1)S(1)}, bf16[512,256]{1,0:T(8,128)(2,1)S(1)}, u32[]{:S(2)}, u32[]{:S(2)}) collective-permute-start(bf16[512,256]{1,0:T(8,128)(2,1)S(1)} %collective-permute-done.5.block_ref), channel_id=1, source_target_pairs={{0,16},{16,32},{32,48},{48,64},{64,80},{80,96},{96,112},{112,128},... | collective-permute-start | bytes 786440 | tf_op jit(solution)/shard_map/ppermute | solution.py:269
  69.8 10.7 %collective-permute-start.7 = (bf16[512,256]{1,0:T(8,128)(2,1)S(1)}, bf16[512,256]{1,0:T(8,128)(2,1)S(1)}, u32[]{:S(2)}, u32[]{:S(2)}) collective-permute-start(bf16[512,256]{1,0:T(8,128)(2,1)S(1)} %collective-permute-done.6.block_ref), channel_id=1, source_target_pairs={{0,16},{16,32},{32,48},{48,64},{64,80},{80,96},{96,112},{112,128},... | collective-permute-start | bytes 786440 | tf_op jit(solution)/shard_map/ppermute | solution.py:269
  80.6 10.7 %collective-permute-start.8 = (bf16[512,256]{1,0:T(8,128)(2,1)S(1)}, bf16[512,256]{1,0:T(8,128)(2,1)S(1)}, u32[]{:S(2)}, u32[]{:S(2)}) collective-permute-start(bf16[512,256]{1,0:T(8,128)(2,1)S(1)} %collective-permute-done.7.block_ref), channel_id=1, source_target_pairs={{0,16},{16,32},{32,48},{48,64},{64,80},{80,96},{96,112},{112,128},... | collective-permute-start | bytes 786440 | tf_op jit(solution)/shard_map/ppermute | solution.py:269
  91.3 10.7 %collective-permute-start.9 = (bf16[512,256]{1,0:T(8,128)(2,1)S(1)}, bf16[512,256]{1,0:T(8,128)(2,1)S(1)}, u32[]{:S(2)}, u32[]{:S(2)}) collective-permute-start(bf16[512,256]{1,0:T(8,128)(2,1)S(1)} %collective-permute-done.8.block_ref), channel_id=1, source_target_pairs={{0,16},{16,32},{32,48},{48,64},{64,80},{80,96},{96,112},{112,128},... | collective-permute-start | bytes 786440 | tf_op jit(solution)/shard_map/ppermute | solution.py:269
  102.0 3.0 %collective-permute-start.10 = (bf16[512,256]{1,0:T(8,128)(2,1)S(1)}, bf16[512,256]{1,0:T(8,128)(2,1)S(1)}, u32[]{:S(2)}, u32[]{:S(2)}) collective-permute-start(bf16[512,256]{1,0:T(8,128)(2,1)S(1)} %collective-permute-done.9.block_ref), channel_id=1, source_target_pairs={{0,16},{16,32},{32,48},{48,64},{64,80},{80,96},{96,112},{112,128},... | collective-permute-start | bytes 786440 | tf_op jit(solution)/shard_map/ppermute | solution.py:269
  105.8 21.9 %collective-permute-start.11 = (f32[4,136,256]{2,1,0:T(8,128)S(1)}, f32[4,136,256]{2,1,0:T(8,128)S(1)}, u32[]{:S(2)}, u32[]{:S(2)}) collective-permute-start(f32[4,136,256]{2,1,0:T(8,128)S(1)} %get-tuple-element.46), channel_id=1, source_target_pairs={{0,8},{8,0},{16,24},{24,16},{32,40},{40,32},{48,56},{56,48},{64,72... | collective-permute-start | bytes 1671176 | tf_op jit(solution)/shard_map/ppermute | solution.py:274

commit v2 on v1

--- a/solution.py
+++ b/solution.py
@@ -21,7 +21,8 @@
 ROWS = SPAN // (CHIPS * CORE)
 KEYS = ROWS * CORE
 PIECE = PREFIX // CHIPS
-BLOCK_ROWS = KEYS + XH * PIECE
+HALF_ROWS = KEYS + PIECE
+BLOCK_ROWS = XH * HALF_ROWS
 LANES = 2 * ROWS
 PARTS = GROUP * ROWS // LANES
 STEPS = Z // 2
@@ -34,22 +35,19 @@
 PARAMS = pltpu.CompilerParams(vmem_limit_bytes=24 * 1024 * 1024)
 
 
-def pack(place_ref, own_ref, first_ref, second_ref, pre_ref, block_ref):
-    core = place_ref[2]
-
-    @pl.when(core == 0)
-    def _():
-        for i, ref in enumerate((own_ref, first_ref)):
-            for j in range(2):
-                block_ref[i * ROWS : (i + 1) * ROWS, j * HD : (j + 1) * HD] = ref[j]
-
-    @pl.when(core != 0)
-    def _():
-        for i, ref in enumerate((first_ref, second_ref)):
-            for j in range(2):
-                block_ref[i * ROWS : (i + 1) * ROWS, j * HD : (j + 1) * HD] = ref[j]
-
-    block_ref[KEYS:, :] = pre_ref[...]
+def lay(keys_ref, vals_ref, pre_keys_ref, pre_vals_ref, span_ref, pre_ref):
+    for i in range(XH * CORE):
+        span_ref[i, :, :HD] = keys_ref[...]
+        span_ref[i, :, HD:] = vals_ref[...]
+        for t in range(TP):
+            pre_ref[i, t, :, :HD] = pre_keys_ref[:, t * HD : (t + 1) * HD]
+            pre_ref[i, t, :, HD:] = pre_vals_ref[:, t * HD : (t + 1) * HD]
+
+
+def pack(span_ref, pre_ref, block_ref):
+    for xh in range(XH):
+        block_ref[xh * HALF_ROWS : xh * HALF_ROWS + KEYS, :] = span_ref[xh * KEYS : (xh + 1) * KEYS, :]
+        block_ref[xh * HALF_ROWS + KEYS : (xh + 1) * HALF_ROWS, :] = pre_ref[xh * PIECE : (xh + 1) * PIECE, :]
 
 
 def plan(place_ref, lengths_ref, seg_ref, q_ref, sib_ref, scalars_ref, bounds_ref, rows_ref):
@@ -108,9 +106,8 @@
         state[:, :, :HD, :] = jnp.zeros((CORE, PARTS, HD, LANES), jnp.float32)
         state[:, :, HD:, :] = jnp.zeros((CORE, PARTS, STATE_ROWS - HD, LANES), jnp.float32)
         state[:, :, HD : HD + 1, :] = jnp.full((CORE, PARTS, 1, LANES), LOW, jnp.float32)
-    core = place_ref[2]
-    chip = place_ref[0] * Z + place_ref[1]
-    origin = lax.rem(jnp.where(core == 0, chip - step + CHIPS, chip + Z + step), CHIPS)
+    core, z = place_ref[2], place_ref[1]
+    origin = lax.rem(jnp.where(core == 0, z - step + Z, z + step), Z)
 
     def absorb(half, row, count, base, kind, masked):
         keys = block_ref[pl.ds(row, count), :HD]
@@ -138,9 +135,9 @@
                 vals, expo.astype(jnp.bfloat16), (((0,), (0,)), ((), ())), preferred_element_type=jnp.float32
             )
 
-    def visit(half, row, count, base, kind, wanted):
+    def visit(half, row, count, base, kind):
         least_lo, most_hi, most_lo, least_hi = [scalars_ref[half * 8 + kind * 4 + i] for i in range(4)]
-        seen = wanted & (base < most_hi) & (base + count > least_lo)
+        seen = (base < most_hi) & (base + count > least_lo)
         whole = (base >= most_lo) & (base + count <= least_hi)
 
         @pl.when(seen & whole)
@@ -151,16 +148,23 @@
         def _():
             absorb(half, row, count, base, kind, True)
 
+    def visit_both(half, xh, row):
+        visit(half, pl.multiple_of(row, PIECE), KEYS, (xh * Z + origin) * KEYS, 1)
+        visit(half, pl.multiple_of(row + KEYS, PIECE), PIECE, (xh * Z + origin) * PIECE, 0)
+
     def one_half(half, carry):
-        visit(half, 0, KEYS, origin * KEYS, 1, (core == 0) | (step < STEPS))
-
-        def one_piece(xh, carry):
-            row = pl.multiple_of(KEYS + xh * PIECE, PIECE)
-            base = (xh * Z + lax.rem(origin, Z)) * PIECE
-            visit(half, row, PIECE, base, 0, (core == 0) | (0 < step < STEPS))
-            return carry
-
-        return lax.fori_loop(0, XH, one_piece, carry)
+        if step == 0:
+            visit_both(half, core, core * HALF_ROWS)
+        elif final:
+            visit_both(half, core, 0)
+        else:
+
+            def one_xh(xh, carry):
+                visit_both(half, xh, xh * HALF_ROWS)
+                return carry
+
+            lax.fori_loop(0, XH, one_xh, 0)
+        return carry
 
     lax.fori_loop(0, CORE, one_half, 0)
     if final:
@@ -185,15 +189,29 @@
 HALF_STATE = jax.ShapeDtypeStruct((PARTS, STATE_ROWS, LANES), jnp.float32)
 
 
-def call_pack(place, own, first, second, pre):
+def call_lay(span_keys, span_values, prefix_keys, prefix_values):
+    return pl.pallas_call(
+        lay,
+        out_shape=(
+            jax.ShapeDtypeStruct((XH * CORE, ROWS, 2 * HD), jnp.bfloat16),
+            jax.ShapeDtypeStruct((XH * CORE, TP, prefix_keys.shape[0], 2 * HD), jnp.bfloat16),
+        ),
+        in_specs=[VMEM] * 4,
+        out_specs=(VMEM, VMEM),
+        compiler_params=PARAMS,
+        name="lay",
+    )(span_keys, span_values, prefix_keys, prefix_values)
+
+
+def call_pack(span, pre):
     return pl.pallas_call(
         pack,
         out_shape=jax.ShapeDtypeStruct((BLOCK_ROWS, 2 * HD), jnp.bfloat16),
-        in_specs=[SMEM, VMEM, VMEM, VMEM, VMEM],
+        in_specs=[VMEM, VMEM],
         out_specs=VMEM,
         compiler_params=PARAMS,
         name="pack",
-    )(place, own, first, second, pre)
+    )(span, pre)
 
 
 def call_plan(place, prefix_lengths, span_seg, queries, sib_queries):
@@ -244,33 +262,29 @@
     place = jnp.stack([lax.axis_index(a) for a in INST]).astype(jnp.int32)
     everyone = [(xh, z) for xh in range(XH) for z in range(Z)]
     cores = [(at(xh, z, c), at(xh, z, 1 - c)) for xh, z in everyone for c in range(CORE)]
-    one = [(at(xh, z, 1), at(xh, z, 0)) for xh, z in everyone] + [(at(xh, z, 0), at(1 - xh, z, 1)) for xh, z in everyone]
-    two = [(at(xh, z, 1), at(1 - xh, z, 1)) for xh, z in everyone]
-    onward = [(c * CORE, (c + 1) % CHIPS * CORE) for c in range(CHIPS)]
-    back = [(c * CORE + 1, (c - 1) % CHIPS * CORE + 1) for c in range(CHIPS)]
-
-    span = jnp.stack([span_keys, span_values])
-    first = lax.ppermute(span, INST, one)
-    second = lax.ppermute(span, INST, two)
-    sib_queries = lax.ppermute(queries, INST, cores)
-
-    pre = jnp.concatenate(
-        [prefix_keys.reshape(-1, KV_HEADS, HD), prefix_values.reshape(-1, KV_HEADS, HD)], axis=2
-    ).transpose(1, 0, 2)
-    pre = jnp.broadcast_to(pre[None], (XH * CORE,) + pre.shape).reshape((XH * CORE * TP,) + pre.shape[1:])
+    along = [(at(xh, z, c), at(xh, (z + 1 - 2 * c) % Z, c)) for xh, z in everyone for c in range(CORE)]
+
+    span, pre = call_lay(span_keys, span_values, prefix_keys, prefix_values)
+    pre = pre.reshape((XH * CORE * TP,) + pre.shape[2:])
     pre = lax.all_to_all(pre, ("xh", "core", "tp"), split_axis=0, concat_axis=0, tiled=True)
-    pre = pre.reshape(XH * PIECE, 2 * HD)
-
-    block = call_pack(place, span, first, second, pre)
-    planned = call_plan(place, prefix_lengths, span_seg, queries, sib_queries)
-    state = None
-    for step in range(STEPS + 1):
-        if step < STEPS:
-            arriving = lax.ppermute(block, INST, onward + back if step < STEPS - 1 else onward)
-        state = call_absorb(step, place, planned, block, state)
-        if step < STEPS:
-            block, state = lax.optimization_barrier((arriving, state))
-    own, sib = state
+    span = lax.all_to_all(span, ("xh", "core"), split_axis=0, concat_axis=0, tiled=True)
+    block = call_pack(span.reshape(XH * KEYS, 2 * HD), pre.reshape(XH * PIECE, 2 * HD))
+
+    own_block, planned, state = block, None, None
+    for step in range(1, STEPS + 1):
+        leaving = block
+        if step == STEPS:
+            leaving = lax.dynamic_slice_in_dim(block, place[2] * HALF_ROWS, HALF_ROWS)
+        arriving = lax.ppermute(leaving, INST, along)
+        if step == 1:
+            planned = call_plan(place, prefix_lengths, span_seg, queries, lax.ppermute(queries, INST, cores))
+            block, planned = lax.optimization_barrier((arriving, planned))
+            continue
+        if step == 2:
+            state = call_absorb(0, place, planned, own_block, state)
+        state = call_absorb(step - 1, place, planned, block, state)
+        block, state = lax.optimization_barrier((arriving, state))
+    own, sib = call_absorb(STEPS, place, planned, block, state)
     return call_merge(own, lax.ppermute(sib, INST, cores))
 
 

time: 129 us -> 128 us (level)
  starting transfers between devices: 94.6 us -> 60.9 us
  blocking collectives: 0 us -> 26.7 us
  waiting for transfers between devices: 12.5 us -> 17.8 us
  local copies, waits for them, and re-layouts: 0.68 us -> 3.02 us
  other arithmetic: 1.64 us -> 0.08 us
    all_to_all x0 -> x2, blocking collectives: none -> 26.7 us  [the longest x1 17.3 us: body(): lax.all_to_all(pre, ('xh', 'core', 'tp'), split_axis=0, concat_axis=0, ti...]
    ppermute x11 -> x9, starting transfers between devices: 63.8 us -> 47.2 us  [the longest x8 45.3 us: body(): arriving = lax.ppermute(leaving, INST, along)]
    all_to_all x1 -> x0, starting transfers between devices: 10.4 us -> none  [body(): lax.all_to_all(pre, ('xh', 'core', 'tp'), split_axis=0, concat_axis=0, ti...]
    ppermute x1, starting transfers between devices: 20.3 us -> 13.7 us  [body(): return call_merge(own, lax.ppermute(sib, INST, cores))]
    ppermute x11 -> x9, waiting for transfers between devices: 11 us -> 16.2 us  [the longest x8 14.8 us: body(): arriving = lax.ppermute(leaving, INST, along)]
    unnamed x6 -> x14, local copies, waits for them, and re-layouts: 0.01 us -> 3 us
  transfers between devices with their start and end apart: 13 -> 10, of which waited for: 9 -> 9; matrix products, arithmetic and copies ran while one was open for 1% -> 0% of each run, Pallas kernels for 13% -> 13%
where the time goes in v2:
time: 128 us; the launch traced here: 127 us
  starting transfers between devices  60.9 us (48%)
  blocking collectives  26.7 us (21%)
  Pallas kernels  18.5 us (14%)
  waiting for transfers between devices  17.8 us (14%)
  local copies, waits for them, and re-layouts  3.02 us (2%)
    ppermute x8, starting transfers between devices, body(): arriving = lax.ppermute(leaving, INST, along)  45.3 us
    all_to_all x1, blocking collectives, body(): lax.all_to_all(pre, ('xh', 'core', 'tp'), split_axis=0, concat_axis=0, ti...  17.3 us
    pallas_call x9, Pallas kernels, call_absorb(): pl.pallas_call(functools.partial(absorb_step, step, final), out_shape=(HA...  16.3 us
    ppermute x8, waiting for transfers between devices, body(): arriving = lax.ppermute(leaving, INST, along)  14.8 us
    ppermute x1, starting transfers between devices, body(): return call_merge(own, lax.ppermute(sib, INST, cores))  13.7 us
    all_to_all x1, blocking collectives, body(): lax.all_to_all(span, ('xh', 'core'), split_axis=0, concat_axis=0, tiled=T...  9.48 us
    unnamed x14, local copies, waits for them, and re-layouts  3 us
  transfers between devices with their start and end apart: 10, of which 9 were waited for; matrix products, arithmetic and copies ran while one was open for 0% of the time, Pallas kernels for 13%

profile of v2, /device:TPU:1, one launch (start us, length us, event | category | flops | bytes accessed | tf_op | source)
XLA Modules:
  0.0 127.3 jit_solution(14306376851168017118)
XLA Ops:
  0.0 0.8 copy-done.1
  0.8 0.8 copy-done.2
  3.1 17.3 %all_to_all.10 = bf16[32,8,256]{2,1,0:T(8,128)(2,1)S(1)} all-to-all(bf16[32,8,256]{2,1,0:T(8,128)(2,1)S(1)} %bitcast.9), channel_id=1, replica_groups=mesh['xh'=2,'z'=16,'core'=2,'tp'=8] {'xh','core','tp'}, dimensions={0} | all-to-all | bytes 262144 | tf_op jit(solution)/shard_map/all_to_all | solution.py:269
  20.3 9.5 %all_to_all.11 = bf16[4,128,256]{2,1,0:T(8,128)(2,1)S(1)} all-to-all(bf16[4,128,256]{2,1,0:T(8,128)(2,1)S(1)} %get-tuple-element.30), channel_id=1, replica_groups=mesh['xh'=2,'z'=16,'core'=2,'tp'=8] {'xh','core'}, dimensions={0} | all-to-all | bytes 524288 | tf_op jit(solution)/shard_map/all_to_all | solution.py:270
  29.8 9.9 %collective-permute-start = (bf16[768,256]{1,0:T(8,128)(2,1)S(1)}, bf16[768,256]{1,0:T(8,128)(2,1)S(1)}, u32[]{:S(2)}, u32[]{:S(2)}) collective-permute-start(bf16[768,256]{1,0:T(8,128)(2,1)S(1)} %pack.1.block_ref), channel_id=1, source_target_pairs={{0,16},{8,248},{16,32},{24,8},{32,48},{40,24},{48,64},{56,40},{64,... | collective-permute-start | bytes 1179656 | tf_op jit(solution)/shard_map/ppermute | solution.py:278
  39.7 1.9 %collective-permute-start.1 = (bf16[128,1024]{1,0:T(8,128)(2,1)S(1)}, bf16[128,1024]{1,0:T(8,128)(2,1)S(1)}, u32[]{:S(2)}, u32[]{:S(2)}) collective-permute-start(bf16[128,1024]{1,0:T(8,128)(2,1)S(1)} %copy-done), channel_id=1, source_target_pairs={{0,8},{8,0},{16,24},{24,16},{32,40},{40,32},{48,56},{56,48},{64,72... | collective-permute-start | bytes 786440 | tf_op jit(solution)/shard_map/ppermute | solution.py:280
  41.8 1.4 %collective-permute-done.1.sib_ref = bf16[128,1024]{1,0:T(8,128)(2,1)S(1)} collective-permute-done((bf16[128,1024]{1,0:T(8,128)(2,1)S(1)}, bf16[128,1024]{1,0:T(8,128)(2,1)S(1)}, u32[]{:S(2)}, u32[]{:S(2)}) %collective-permute-start.1) | collective-permute-done | bytes 262176 | tf_op jit(solution)/shard_map/ppermute | solution.py:280
  43.2 1.3 %plan.1 = (s32[16]{0:T(128)S(1)}, s32[2,8,128]{2,1,0:T(8,128)S(1)}, bf16[2,4,256,128]{3,2,1,0:T(8,128)(2,1)S(1)}) custom-call(s32[3]{0:T(128)S(1)} %pad_add_fusion.place_ref, s32[4]{0:T(128)S(1)} %copy-done.6, s32[64,128]{1,0:T(8,128)S(1)} %bitcast.10, bf16[128,1024]{1,0:T(8,128)(2,1)S(1)} %copy-done, bf16[128,1024]{1,0:T(8,128)(2,1)S(1)} %collective-permute-done.1.sib_ref), custom_call_target="tpu_custom_call" | custom-call | tf_op jit(solution)/shard_map/plan/pallas_call | solution.py:218
  44.5 4.9 %collective-permute-start.2 = (bf16[768,256]{1,0:T(8,128)(2,1)S(1)}, bf16[768,256]{1,0:T(8,128)(2,1)S(1)}, u32[]{:S(2)}, u32[]{:S(2)}) collective-permute-start(bf16[768,256]{1,0:T(8,128)(2,1)S(1)} %collective-permute-done.block_ref), channel_id=1, source_target_pairs={{0,16},{8,248},{16,32},{24,8},{32,48},{40,24},{48,64},{56,40},{64,... | collective-permute-start | bytes 1179656 | tf_op jit(solution)/shard_map/ppermute | solution.py:278
  50.2 2.1 %absorb.10.refs_0_ = f32[2,4,136,256]{3,2,1,0:T(8,128)S(1)} custom-call(s32[3]{0:T(128)S(1)} %pad_add_fusion.place_ref, s32[16]{0:T(128)S(1)} %get-tuple-element.35.scalars_ref, s32[2,8,128]{2,1,0:T(8,128)S(1)} %get-tuple-element.36.bounds_ref, bf16[2,4,256,128]{3,2,1,0:T(8,128)(2,1)S(1)} %get-tuple-element.37.rows_ref, ...), custom_call_target="tpu_custom_call" | custom-call | flops 537000000 | bytes 3000000 | tf_op jit(solution)/shard_map/absorb/pallas_call | solution.py:234
  52.3 1.9 %collective-permute-done.2.block_ref = bf16[768,256]{1,0:T(8,128)(2,1)S(1)} collective-permute-done((bf16[768,256]{1,0:T(8,128)(2,1)S(1)}, bf16[768,256]{1,0:T(8,128)(2,1)S(1)}, u32[]{:S(2)}, u32[]{:S(2)}) %collective-permute-start.2) | collective-permute-done | bytes 393248 | tf_op jit(solution)/shard_map/ppermute | solution.py:278
  54.2 5.0 %collective-permute-start.3 = (bf16[768,256]{1,0:T(8,128)(2,1)S(1)}, bf16[768,256]{1,0:T(8,128)(2,1)S(1)}, u32[]{:S(2)}, u32[]{:S(2)}) collective-permute-start(bf16[768,256]{1,0:T(8,128)(2,1)S(1)} %collective-permute-done.2.block_ref), channel_id=1, source_target_pairs={{0,16},{8,248},{16,32},{24,8},{32,48},{40,24},{48,64},{56,40},{64,... | collective-permute-start | bytes 1179656 | tf_op jit(solution)/shard_map/ppermute | solution.py:278
  59.2 2.1 %absorb.11.refs_0_ = f32[2,4,136,256]{3,2,1,0:T(8,128)S(1)} custom-call(s32[3]{0:T(128)S(1)} %pad_add_fusion.place_ref, s32[16]{0:T(128)S(1)} %get-tuple-element.35.scalars_ref, s32[2,8,128]{2,1,0:T(8,128)S(1)} %get-tuple-element.36.bounds_ref, bf16[2,4,256,128]{3,2,1,0:T(8,128)(2,1)S(1)} %get-tuple-element.37.rows_ref, ...), custom_call_target="tpu_custom_call" | custom-call | flops 537000000 | bytes 3000000 | tf_op jit(solution)/shard_map/absorb/pallas_call | solution.py:234
  61.3 2.6 %collective-permute-done.3.block_ref = bf16[768,256]{1,0:T(8,128)(2,1)S(1)} collective-permute-done((bf16[768,256]{1,0:T(8,128)(2,1)S(1)}, bf16[768,256]{1,0:T(8,128)(2,1)S(1)}, u32[]{:S(2)}, u32[]{:S(2)}) %collective-permute-start.3) | collective-permute-done | bytes 393248 | tf_op jit(solution)/shard_map/ppermute | solution.py:278
  63.9 5.0 %collective-permute-start.4 = (bf16[768,256]{1,0:T(8,128)(2,1)S(1)}, bf16[768,256]{1,0:T(8,128)(2,1)S(1)}, u32[]{:S(2)}, u32[]{:S(2)}) collective-permute-start(bf16[768,256]{1,0:T(8,128)(2,1)S(1)} %collective-permute-done.3.block_ref), channel_id=1, source_target_pairs={{0,16},{8,248},{16,32},{24,8},{32,48},{40,24},{48,64},{56,40},{64,... | collective-permute-start | bytes 1179656 | tf_op jit(solution)/shard_map/ppermute | solution.py:278
  68.9 2.1 %absorb.12.refs_0_ = f32[2,4,136,256]{3,2,1,0:T(8,128)S(1)} custom-call(s32[3]{0:T(128)S(1)} %pad_add_fusion.place_ref, s32[16]{0:T(128)S(1)} %get-tuple-element.35.scalars_ref, s32[2,8,128]{2,1,0:T(8,128)S(1)} %get-tuple-element.36.bounds_ref, bf16[2,4,256,128]{3,2,1,0:T(8,128)(2,1)S(1)} %get-tuple-element.37.rows_ref, ...), custom_call_target="tpu_custom_call" | custom-call | flops 537000000 | bytes 3000000 | tf_op jit(solution)/shard_map/absorb/pallas_call | solution.py:234
  71.0 2.6 %collective-permute-done.4.block_ref = bf16[768,256]{1,0:T(8,128)(2,1)S(1)} collective-permute-done((bf16[768,256]{1,0:T(8,128)(2,1)S(1)}, bf16[768,256]{1,0:T(8,128)(2,1)S(1)}, u32[]{:S(2)}, u32[]{:S(2)}) %collective-permute-start.4) | collective-permute-done | bytes 393248 | tf_op jit(solution)/shard_map/ppermute | solution.py:278
  73.6 5.2 %collective-permute-start.5 = (bf16[768,256]{1,0:T(8,128)(2,1)S(1)}, bf16[768,256]{1,0:T(8,128)(2,1)S(1)}, u32[]{:S(2)}, u32[]{:S(2)}) collective-permute-start(bf16[768,256]{1,0:T(8,128)(2,1)S(1)} %collective-permute-done.4.block_ref), channel_id=1, source_target_pairs={{0,16},{8,248},{16,32},{24,8},{32,48},{40,24},{48,64},{56,40},{64,... | collective-permute-start | bytes 1179656 | tf_op jit(solution)/shard_map/ppermute | solution.py:278
  78.8 2.1 %absorb.13.refs_0_ = f32[2,4,136,256]{3,2,1,0:T(8,128)S(1)} custom-call(s32[3]{0:T(128)S(1)} %pad_add_fusion.place_ref, s32[16]{0:T(128)S(1)} %get-tuple-element.35.scalars_ref, s32[2,8,128]{2,1,0:T(8,128)S(1)} %get-tuple-element.36.bounds_ref, bf16[2,4,256,128]{3,2,1,0:T(8,128)(2,1)S(1)} %get-tuple-element.37.rows_ref, ...), custom_call_target="tpu_custom_call" | custom-call | flops 537000000 | bytes 3000000 | tf_op jit(solution)/shard_map/absorb/pallas_call | solution.py:234
  80.9 2.4 %collective-permute-done.5.block_ref = bf16[768,256]{1,0:T(8,128)(2,1)S(1)} collective-permute-done((bf16[768,256]{1,0:T(8,128)(2,1)S(1)}, bf16[768,256]{1,0:T(8,128)(2,1)S(1)}, u32[]{:S(2)}, u32[]{:S(2)}) %collective-permute-start.5) | collective-permute-done | bytes 393248 | tf_op jit(solution)/shard_map/ppermute | solution.py:278
  83.3 5.0 %collective-permute-start.6 = (bf16[768,256]{1,0:T(8,128)(2,1)S(1)}, bf16[768,256]{1,0:T(8,128)(2,1)S(1)}, u32[]{:S(2)}, u32[]{:S(2)}) collective-permute-start(bf16[768,256]{1,0:T(8,128)(2,1)S(1)} %collective-permute-done.5.block_ref), channel_id=1, source_target_pairs={{0,16},{8,248},{16,32},{24,8},{32,48},{40,24},{48,64},{56,40},{64,... | collective-permute-start | bytes 1179656 | tf_op jit(solution)/shard_map/ppermute | solution.py:278
  88.3 2.1 %absorb.14.refs_0_ = f32[2,4,136,256]{3,2,1,0:T(8,128)S(1)} custom-call(s32[3]{0:T(128)S(1)} %pad_add_fusion.place_ref, s32[16]{0:T(128)S(1)} %get-tuple-element.35.scalars_ref, s32[2,8,128]{2,1,0:T(8,128)S(1)} %get-tuple-element.36.bounds_ref, bf16[2,4,256,128]{3,2,1,0:T(8,128)(2,1)S(1)} %get-tuple-element.37.rows_ref, ...), custom_call_target="tpu_custom_call" | custom-call | flops 537000000 | bytes 3000000 | tf_op jit(solution)/shard_map/absorb/pallas_call | solution.py:234
  90.5 2.6 %collective-permute-done.6.block_ref = bf16[768,256]{1,0:T(8,128)(2,1)S(1)} collective-permute-done((bf16[768,256]{1,0:T(8,128)(2,1)S(1)}, bf16[768,256]{1,0:T(8,128)(2,1)S(1)}, u32[]{:S(2)}, u32[]{:S(2)}) %collective-permute-start.6) | collective-permute-done | bytes 393248 | tf_op jit(solution)/shard_map/ppermute | solution.py:278
  93.0 5.0 %collective-permute-start.7 = (bf16[768,256]{1,0:T(8,128)(2,1)S(1)}, bf16[768,256]{1,0:T(8,128)(2,1)S(1)}, u32[]{:S(2)}, u32[]{:S(2)}) collective-permute-start(bf16[768,256]{1,0:T(8,128)(2,1)S(1)} %collective-permute-done.6.block_ref), channel_id=1, source_target_pairs={{0,16},{8,248},{16,32},{24,8},{32,48},{40,24},{48,64},{56,40},{64,... | collective-permute-start | bytes 1179656 | tf_op jit(solution)/shard_map/ppermute | solution.py:278
  98.1 2.1 %absorb.15.refs_0_ = f32[2,4,136,256]{3,2,1,0:T(8,128)S(1)} custom-call(s32[3]{0:T(128)S(1)} %pad_add_fusion.place_ref, s32[16]{0:T(128)S(1)} %get-tuple-element.35.scalars_ref, s32[2,8,128]{2,1,0:T(8,128)S(1)} %get-tuple-element.36.bounds_ref, bf16[2,4,256,128]{3,2,1,0:T(8,128)(2,1)S(1)} %get-tuple-element.37.rows_ref, ...), custom_call_target="tpu_custom_call" | custom-call | flops 537000000 | bytes 3000000 | tf_op jit(solution)/shard_map/absorb/pallas_call | solution.py:234
  100.2 2.6 %collective-permute-done.7.block_ref = bf16[768,256]{1,0:T(8,128)(2,1)S(1)} collective-permute-done((bf16[768,256]{1,0:T(8,128)(2,1)S(1)}, bf16[768,256]{1,0:T(8,128)(2,1)S(1)}, u32[]{:S(2)}, u32[]{:S(2)}) %collective-permute-start.7) | collective-permute-done | bytes 393248 | tf_op jit(solution)/shard_map/ppermute | solution.py:278
  102.8 5.2 %collective-permute-start.8 = (bf16[384,256]{1,0:T(8,128)(2,1)S(1)}, bf16[384,256]{1,0:T(8,128)(2,1)S(1)}, u32[]{:S(2)}, u32[]{:S(2)}) collective-permute-start(bf16[384,256]{1,0:T(8,128)(2,1)S(1)} %constant_dynamic-slice_fusion), channel_id=1, source_target_pairs={{0,16},{8,248},{16,32},{24,8},{32,48},{40,24},{48,64},{56,40},{64,... | collective-permute-start | bytes 589832 | tf_op jit(solution)/shard_map/ppermute | solution.py:278
  108.0 2.1 %absorb.16.refs_0_ = f32[2,4,136,256]{3,2,1,0:T(8,128)S(1)} custom-call(s32[3]{0:T(128)S(1)} %pad_add_fusion.place_ref, s32[16]{0:T(128)S(1)} %get-tuple-element.35.scalars_ref, s32[2,8,128]{2,1,0:T(8,128)S(1)} %get-tuple-element.36.bounds_ref, bf16[2,4,256,128]{3,2,1,0:T(8,128)(2,1)S(1)} %get-tuple-element.37.rows_ref, ...), custom_call_target="tpu_custom_call" | custom-call | flops 537000000 | bytes 3000000 | tf_op jit(solution)/shard_map/absorb/pallas_call | solution.py:234
  110.4 0.8 absorb.17
  111.2 13.7 %collective-permute-start.9 = (f32[4,136,256]{2,1,0:T(8,128)S(1)}, f32[4,136,256]{2,1,0:T(8,128)S(1)}, u32[]{:S(2)}, u32[]{:S(2)}) collective-permute-start(f32[4,136,256]{2,1,0:T(8,128)S(1)} %get-tuple-element.54), channel_id=1, source_target_pairs={{0,8},{8,0},{16,24},{24,16},{32,40},{40,32},{48,56},{56,48},{64,72... | collective-permute-start | bytes 1671176 | tf_op jit(solution)/shard_map/ppermute | solution.py:288
  124.8 1.6 %collective-permute-done.9.other_ref = f32[4,136,256]{2,1,0:T(8,128)S(1)} collective-permute-done((f32[4,136,256]{2,1,0:T(8,128)S(1)}, f32[4,136,256]{2,1,0:T(8,128)S(1)}, u32[]{:S(2)}, u32[]{:S(2)}) %collective-permute-start.9) | collective-permute-done | bytes 557088 | tf_op jit(solution)/shard_map/ppermute | solution.py:288
  126.4 0.9 merge.1
  (19 shorter events, 2.6 us)
Async XLA Ops:
  0.0 39.7 %copy-start = (bf16[128,1024]{1,0:T(8,128)(2,1)S(1)}, bf16[128,1024]{1,0:T(8,128)(2,1)}, u32[]{:S(2)}) copy-start(bf16[128,1024]{1,0:T(8,128)(2,1)} %q_ref.1) | copy-start | bytes 786436
  0.0 0.8 copy-start.1
  0.8 0.8 copy-start.2
  1.6 0.7 copy-start.4
  2.3 0.7 copy-start.5
  3.0 40.2 %copy-start.3 = (s32[8192]{0:T(1024)S(1)}, s32[8192]{0:T(1024)}, u32[]{:S(2)}) copy-start(s32[8192]{0:T(1024)} %param.12) | copy-start | bytes 98308
  3.0 40.2 %copy-start.6 = (s32[4]{0:T(128)S(1)}, s32[4]{0:T(128)}, u32[]{:S(2)}) copy-start(s32[4]{0:T(128)} %lengths_ref.1) | copy-start | bytes 52
  29.8 14.7 %collective-permute-start = (bf16[768,256]{1,0:T(8,128)(2,1)S(1)}, bf16[768,256]{1,0:T(8,128)(2,1)S(1)}, u32[]{:S(2)}, u32[]{:S(2)}) collective-permute-start(bf16[768,256]{1,0:T(8,128)(2,1)S(1)} %pack.1.block_ref), channel_id=1, source_target_pairs={{0,16},{8,248},{16,32},{24,8},{32,48},{40,24},{48,64},{56,40},{64,... | collective-permute-start | bytes 1179656 | tf_op jit(solution)/shard_map/ppermute | solution.py:278
  39.7 3.4 %collective-permute-start.1 = (bf16[128,1024]{1,0:T(8,128)(2,1)S(1)}, bf16[128,1024]{1,0:T(8,128)(2,1)S(1)}, u32[]{:S(2)}, u32[]{:S(2)}) collective-permute-start(bf16[128,1024]{1,0:T(8,128)(2,1)S(1)} %copy-done), channel_id=1, source_target_pairs={{0,8},{8,0},{16,24},{24,16},{32,40},{40,32},{48,56},{56,48},{64,72... | collective-permute-start | bytes 786440 | tf_op jit(solution)/shard_map/ppermute | solution.py:280
  44.5 9.7 %collective-permute-start.2 = (bf16[768,256]{1,0:T(8,128)(2,1)S(1)}, bf16[768,256]{1,0:T(8,128)(2,1)S(1)}, u32[]{:S(2)}, u32[]{:S(2)}) collective-permute-start(bf16[768,256]{1,0:T(8,128)(2,1)S(1)} %collective-permute-done.block_ref), channel_id=1, source_target_pairs={{0,16},{8,248},{16,32},{24,8},{32,48},{40,24},{48,64},{56,40},{64,... | collective-permute-start | bytes 1179656 | tf_op jit(solution)/shard_map/ppermute | solution.py:278
  54.2 9.7 %collective-permute-start.3 = (bf16[768,256]{1,0:T(8,128)(2,1)S(1)}, bf16[768,256]{1,0:T(8,128)(2,1)S(1)}, u32[]{:S(2)}, u32[]{:S(2)}) collective-permute-start(bf16[768,256]{1,0:T(8,128)(2,1)S(1)} %collective-permute-done.2.block_ref), channel_id=1, source_target_pairs={{0,16},{8,248},{16,32},{24,8},{32,48},{40,24},{48,64},{56,40},{64,... | collective-permute-start | bytes 1179656 | tf_op jit(solution)/shard_map/ppermute | solution.py:278
  63.9 9.7 %collective-permute-start.4 = (bf16[768,256]{1,0:T(8,128)(2,1)S(1)}, bf16[768,256]{1,0:T(8,128)(2,1)S(1)}, u32[]{:S(2)}, u32[]{:S(2)}) collective-permute-start(bf16[768,256]{1,0:T(8,128)(2,1)S(1)} %collective-permute-done.3.block_ref), channel_id=1, source_target_pairs={{0,16},{8,248},{16,32},{24,8},{32,48},{40,24},{48,64},{56,40},{64,... | collective-permute-start | bytes 1179656 | tf_op jit(solution)/shard_map/ppermute | solution.py:278
  73.6 9.7 %collective-permute-start.5 = (bf16[768,256]{1,0:T(8,128)(2,1)S(1)}, bf16[768,256]{1,0:T(8,128)(2,1)S(1)}, u32[]{:S(2)}, u32[]{:S(2)}) collective-permute-start(bf16[768,256]{1,0:T(8,128)(2,1)S(1)} %collective-permute-done.4.block_ref), channel_id=1, source_target_pairs={{0,16},{8,248},{16,32},{24,8},{32,48},{40,24},{48,64},{56,40},{64,... | collective-permute-start | bytes 1179656 | tf_op jit(solution)/shard_map/ppermute | solution.py:278
  83.3 9.7 %collective-permute-start.6 = (bf16[768,256]{1,0:T(8,128)(2,1)S(1)}, bf16[768,256]{1,0:T(8,128)(2,1)S(1)}, u32[]{:S(2)}, u32[]{:S(2)}) collective-permute-start(bf16[768,256]{1,0:T(8,128)(2,1)S(1)} %collective-permute-done.5.block_ref), channel_id=1, source_target_pairs={{0,16},{8,248},{16,32},{24,8},{32,48},{40,24},{48,64},{56,40},{64,... | collective-permute-start | bytes 1179656 | tf_op jit(solution)/shard_map/ppermute | solution.py:278
  93.0 9.7 %collective-permute-start.7 = (bf16[768,256]{1,0:T(8,128)(2,1)S(1)}, bf16[768,256]{1,0:T(8,128)(2,1)S(1)}, u32[]{:S(2)}, u32[]{:S(2)}) collective-permute-start(bf16[768,256]{1,0:T(8,128)(2,1)S(1)} %collective-permute-done.6.block_ref), channel_id=1, source_target_pairs={{0,16},{8,248},{16,32},{24,8},{32,48},{40,24},{48,64},{56,40},{64,... | collective-permute-start | bytes 1179656 | tf_op jit(solution)/shard_map/ppermute | solution.py:278
  102.8 7.6 %collective-permute-start.8 = (bf16[384,256]{1,0:T(8,128)(2,1)S(1)}, bf16[384,256]{1,0:T(8,128)(2,1)S(1)}, u32[]{:S(2)}, u32[]{:S(2)}) collective-permute-start(bf16[384,256]{1,0:T(8,128)(2,1)S(1)} %constant_dynamic-slice_fusion), channel_id=1, source_target_pairs={{0,16},{8,248},{16,32},{24,8},{32,48},{40,24},{48,64},{56,40},{64,... | collective-permute-start | bytes 589832 | tf_op jit(solution)/shard_map/ppermute | solution.py:278
  111.2 15.2 %collective-permute-start.9 = (f32[4,136,256]{2,1,0:T(8,128)S(1)}, f32[4,136,256]{2,1,0:T(8,128)S(1)}, u32[]{:S(2)}, u32[]{:S(2)}) collective-permute-start(f32[4,136,256]{2,1,0:T(8,128)S(1)} %get-tuple-element.54), channel_id=1, source_target_pairs={{0,8},{8,0},{16,24},{24,16},{32,40},{40,32},{48,56},{56,48},{64,72... | collective-permute-start | bytes 1671176 | tf_op jit(solution)/shard_map/ppermute | solution.py:288
